TPU v7x, 512 devices: a whole 4x8x8 slice. The times are simulated.
512 devices in a mesh: rec: 16 (over z, core), frame: 32 (over x, y).
Axes of the slice: x: 4, y: 8, z: 8, core: 2. Of those that a mesh axis runs over, the one named last changes fastest.
Arguments:
- frames: bfloat16 [16, 49152, 256], P('rec', 'frame'), may hold values from -10 to 10
- texts: bfloat16 [32, 224, 256], P('rec', 'frame'), may hold values from -100 to 100
- pair_rec: int32 [32, 1], replicated, may hold values from 0 to 15, as said below
- pair_text: int32 [32], replicated, may hold values from 0 to 31, as said below
- pair_label: int32 [32], replicated, may hold values 0 or 1
Outputs:
- loss: float32 [], replicated
- grad_frames: bfloat16 [16, 49152, 256], P('rec', 'frame')
- grad_texts: bfloat16 [32, 224, 256], P('rec', 'frame')
Inputs may be any that keep to these rules, and one draw needn't show every extreme that they name: `pair_rec`: no recording is named by more than 6 pairs, some recording by exactly 6, and every recording by at least one. A pair's text is held by the index of rec one after, one before, or 8 after its recording (counted round): pair_text // 2 = (pair_rec + k) mod 16 with k one of 1, 15, 8.
All inputs are finite; a program needn't handle non-finite values.
Results may differ from a plain program's by a relative error of at most 0.0085.
Values may be sent and summed in bfloat16 or wider, within the bound.
A program may use at most 64 MiB of HBM per device.

v0:
```python
import jax
import jax.numpy as jnp
from jax import lax
from jax.sharding import PartitionSpec as P

MOST = 6
EPS = 1e-06
TEMP = 10.0
BIAS = -1.0
LOSS_SCALE = 2048.0


def slot_tables(pair_rec, pair_text, pair_label, here, most):
    record = pair_rec[:, 0]
    count = record.shape[0]
    order = jnp.arange(count, dtype=jnp.int32)
    same = (record[:, None] == record[None, :]).astype(jnp.int32)
    earlier = (order[None, :] < order[:, None]).astype(jnp.int32)
    rank = jnp.sum(same * earlier, axis=1)
    places = jnp.arange(most, dtype=jnp.int32)
    chosen = ((record[None, :] == here) & (rank[None, :] == places[:, None])).astype(jnp.int32)
    valid = jnp.sum(chosen, axis=1)
    slot_text = jnp.sum(chosen * pair_text[None, :], axis=1)
    sign = jnp.sum(chosen * (2 * pair_label[None, :] - 1), axis=1)
    return (valid, slot_text, sign)


def pair_terms(score, valid, sign, tokens):
    margin = -sign * (TEMP * score + BIAS)
    loss_part = valid * jax.nn.softplus(margin)
    grad_cos = -LOSS_SCALE * TEMP * valid * sign * jax.nn.sigmoid(margin) / tokens
    return (loss_part, grad_cos)


def body(frames, texts, pair_rec, pair_text, pair_label):
    here = lax.axis_index("rec")
    part = lax.axis_index("frame")
    owned, width_rows, width = texts.shape
    tokens = width_rows * lax.axis_size("frame")
    n_text = owned * lax.axis_size("rec")
    valid, slot_text, sign = slot_tables(pair_rec, pair_text, pair_label, here, MOST)
    valid_f = valid.astype(jnp.float32)
    sign_f = sign.astype(jnp.float32)
    picks = (
        (slot_text[:, None] == jnp.arange(n_text, dtype=jnp.int32)[None, :]) & (valid[:, None] > 0)
    ).astype(jnp.bfloat16)
    whole = lax.all_gather(texts, "frame", axis=1, tiled=True)
    query_vectors = jnp.einsum(
        "jc,cgx->jgx",
        picks,
        lax.all_gather(whole, "rec", axis=0, tiled=True),
        preferred_element_type=jnp.float32,
    ).astype(jnp.bfloat16)
    upstream_signal = frames[0]
    logit_scale = width ** (-0.5)
    pair_scores = (
        jnp.einsum(
            "ype,je->ypj", query_vectors, upstream_signal, preferred_element_type=jnp.float32
        )
        * logit_scale
    )
    local_max = jnp.max(pair_scores, axis=2)
    row_max = lax.pmax(local_max, "frame")
    expo = jnp.exp(pair_scores - row_max[..., None])
    batch_weights = expo.astype(jnp.bfloat16)
    value_partial = jnp.einsum(
        "pqx,xh->pqh", batch_weights, upstream_signal, preferred_element_type=jnp.float32
    )
    query_f = query_vectors.astype(jnp.float32)
    q_norm = lax.rsqrt(jnp.sum(query_f * query_f, axis=2) + EPS)
    q_unit = query_f * q_norm[..., None]
    context = lax.psum(value_partial, "frame")
    c_norm = lax.rsqrt(jnp.sum(context * context, axis=2) + EPS)
    c_unit = context * c_norm[..., None]
    cos = jnp.sum(q_unit * c_unit, axis=2)
    score = jnp.mean(cos, axis=1)
    loss_part, grad_cos = pair_terms(score, valid_f, sign_f, tokens)
    weight = grad_cos[:, None, None]
    d_context = weight * (q_unit - cos[..., None] * c_unit) * c_norm[..., None]
    direct = weight * (c_unit - cos[..., None] * q_unit) * q_norm[..., None]
    direct_own = lax.dynamic_slice_in_dim(direct, part * width_rows, width_rows, 1)
    context_batch_gradient = d_context.astype(jnp.bfloat16)
    weight_gradient = jnp.einsum(
        "ype,je->ypj", context_batch_gradient, upstream_signal, preferred_element_type=jnp.float32
    )
    score_gradient = (expo * weight_gradient * logit_scale).astype(jnp.bfloat16)
    d_query = lax.psum_scatter(
        jnp.einsum(
            "slf,fd->lsd", score_gradient, upstream_signal, preferred_element_type=jnp.float32
        ),
        "frame",
        scatter_dimension=0,
        tiled=True,
    )
    d_query = d_query + jnp.transpose(direct_own, (1, 0, 2))
    text_term = jnp.einsum(
        "st,lsd->tld", picks.astype(jnp.float32), d_query, precision=lax.Precision.HIGHEST
    )
    grad_texts = lax.psum_scatter(text_term, "rec", scatter_dimension=0, tiled=True).astype(
        jnp.bfloat16
    )
    frame_loss_piece = jnp.einsum(
        "cvm,cvz->mz", score_gradient, query_vectors, preferred_element_type=jnp.float32
    )
    frame_loss_piece = frame_loss_piece + jnp.einsum(
        "cvm,cvz->mz", batch_weights, context_batch_gradient, preferred_element_type=jnp.float32
    )
    grad_frames = frame_loss_piece.astype(jnp.bfloat16)[None]
    loss = lax.psum(jnp.sum(loss_part), "rec")
    return (loss, grad_frames, grad_texts)


def solution(mesh):
    return jax.shard_map(
        body,
        mesh=mesh,
        in_specs=(P("rec", "frame", None), P("rec", "frame", None), P(), P(), P()),
        out_specs=(P(), P("rec", "frame", None), P("rec", "frame", None)),
        check_vma=False,
    )
```

profile of v0, /device:TPU:16, one launch (start us, length us, event | category | flops | bytes accessed | tf_op | source)
XLA Modules:
  0.0 644.4 jit_solution(15901261809968272552)
XLA Ops:
  7.2 49.8 %all_gather.6 = bf16[2,224,256]{2,0,1:T(2,128)(2,1)S(1)} all-gather(bf16[2,7,256]{2,0,1:T(2,128)(2,1)} %param.6), channel_id=1, replica_groups=mesh['rec'=16,'frame'=32] {'frame'}, dimensions={1}, use_global_device_ids=true | all-gather | bytes 236544 | tf_op jit(solution)/shard_map/all_gather | solution.py:47
  57.0 0.7 copy.20
  57.8 0.9 select_reduce_fusion
  58.7 0.7 broadcast_compare_fusion.1
  59.4 0.7 multiply_add_fusion
  60.1 1.3 select_reduce_fusion.2
  61.4 43.4 %all-gather.2.cloned.1.call-done = bf16[32,224,256]{2,1,0:T(8,128)(2,1)} async-done(((bf16[2,224,256]{2,1,0:T(8,128)(2,1)}), bf16[32,224,256]{2,1,0:T(8,128)(2,1)}) %all-gather.2.cloned.1.call-update) | async-done | bytes 3670032 | tf_op jit(solution)/shard_map/all_gather | solution.py:51
  104.7 4.3 fusion.6
  109.0 4.4 multiply_reduce_fusion
  113.4 71.4 %pmax.7 = f32[6,224]{1,0:T(8,128)S(1)} all-reduce(f32[6,224]{1,0:T(8,128)S(1)} %get-tuple-element.17), channel_id=1, replica_groups=mesh['rec'=16,'frame'=32] {'frame'}, use_global_device_ids=true, to_apply=%region_6.0 | all-reduce | flops 1344 | bytes 10752 | tf_op jit(solution)/shard_map/pmax | solution.py:63
  184.8 4.9 fusion.13
  189.7 2.1 copy.23
  191.8 0.2 reduce-scatter.3.cloned.1.call-start
  192.0 0.7 add_rsqrt_fusion.1
  192.6 157.1 %all-reduce.5.cloned.1.call-done = f32[6,224,256]{2,0,1:T(8,128)} async-done(((f32[6,224,256]{2,0,1:T(8,128)}), f32[6,224,256]{2,0,1:T(8,128)}) %all-reduce.5.cloned.1.call-update) | async-done | bytes 1376272 | tf_op jit(solution)/shard_map/psum | solution.py:72
  349.7 1.9 multiply_reduce_fusion.1
  351.6 2.4 multiply_reduce_fusion.2
  354.0 1.4 fusion.44
  355.4 1.8 convert_multiply_fusion
  357.2 4.9 multiply_convert_fusion
  362.2 1.3 fusion.10
  363.5 0.7 copy-done.10
  364.2 2.1 copy.47
  366.2 1.3 dynamic-slice
  368.2 0.7 constant_dynamic-slice_fusion
  368.9 0.7 constant_dynamic-slice_fusion.1
  369.6 5.7 convolution_bitcast_fusion
  375.3 2.3 fusion.5
  377.6 209.2 %reduce-scatter.3.cloned.1.call-done = f32[7,6,256]{2,1,0:T(8,128)} async-done(((f32[224,6,256]{2,1,0:T(8,128)}), f32[7,6,256]{2,1,0:T(8,128)}) %reduce-scatter.3.cloned.1.call-update) | async-done | bytes 43024 | tf_op jit(solution)/shard_map/reduce_scatter | solution.py:87
  586.9 1.3 fusion.27
  588.2 49.1 %all-reduce.6 = (f32[]{:T(128)}, bf16[32,7,256]{2,0,1:T(8,128)(2,1)S(1)}) all-reduce(f32[]{:T(128)} %get-tuple-element.14, f32[32,7,256]{2,0,1:T(8,128)S(1)} %fusion.27), channel_id=1, replica_groups=mesh['rec'=16,'frame'=32] {'rec'}, use_global_device_ids=true, to_apply=%region_11.12 | all-reduce | flops 57345 | bytes 344072 | tf_op jit(solution)/shard_map/psum | solution.py:109
  637.3 0.6 dynamic-slice_convert_fusion
  (30 shorter events, 0.2 us)
Async XLA Ops:
  7.2 101.8 %copy-start = (bf16[1,1536,256]{2,1,0:T(8,128)(2,1)S(1)}, bf16[1,1536,256]{2,1,0:T(8,128)(2,1)}, u32[]{:S(2)}) copy-start(bf16[1,1536,256]{2,1,0:T(8,128)(2,1)} %param.5) | copy-start | bytes 2359300
  7.2 97.5 %all-gather.2.cloned.1.call-start = ((), (), s32[]{:S(2)}) async-start(), calls=%async_computation.1 | async-start | bytes 3899392 | tf_op jit(solution)/shard_map/all_gather | solution.py:51
  57.8 291.9 %all-reduce.5.cloned.1.call-start = ((), (), s32[]{:S(2)}) async-start(), calls=%async_computation.2 | async-start | bytes 3670016 | tf_op jit(solution)/shard_map/psum | solution.py:72
  61.3 43.4 %copy-start.9 = (s32[6]{0:T(128)}, s32[6]{0:T(128)S(1)}, u32[]{:S(2)}) copy-start(s32[6]{0:T(128)S(1)} %get-tuple-element.7) | copy-start | bytes 76
  61.3 47.6 %copy-start.4 = (s32[6]{0:T(128)}, s32[6]{0:T(128)S(1)}, u32[]{:S(2)}) copy-start(s32[6]{0:T(128)S(1)} %get-tuple-element.6) | copy-start | bytes 76
  61.4 47.6 %copy-start.8 = (pred[6]{0:T(512)(128)(4,1)}, pred[6]{0:T(512)(128)(4,1)S(1)}, u32[]{:S(2)}) copy-start(pred[6]{0:T(512)(128)(4,1)S(1)} %broadcast_compare_fusion) | copy-start | bytes 22
  191.8 395.1 %reduce-scatter.3.cloned.1.call-start = ((), (), s32[]{:S(2)}) async-start(), calls=%async_computation.3 | async-start | bytes 1892352 | tf_op jit(solution)/shard_map/reduce_scatter | solution.py:87
  349.7 5.7 copy-start.1
  354.0 3.2 copy-start.3
  355.4 6.8 %copy-start.6 = (f32[6]{0:T(128)}, f32[6]{0:T(128)S(1)}, u32[]{:S(2)}) copy-start(f32[6]{0:T(128)S(1)} %get-tuple-element.13) | copy-start | bytes 76
  357.2 5.0 copy-start.2
  362.2 2.0 copy-start.10
  369.6 5.7 copy-start.11
  375.3 211.6 %copy-start.5 = (s32[6]{0:T(128)S(1)}, s32[6]{0:T(128)}, u32[]{:S(2)}) copy-start(s32[6]{0:T(128)} %copy-done.4) | copy-start | bytes 76
  375.3 211.6 %copy-start.7 = (f32[6]{0:T(128)S(1)}, f32[6]{0:T(128)}, u32[]{:S(2)}) copy-start(f32[6]{0:T(128)} %copy-done.6) | copy-start | bytes 76
Sparse Core Ops, SparseCore 0:
  57.9 46.7 all-gather.1
  191.9 157.7 all-reduce.4
  366.4 220.4 reduce-scatter.2
where the time goes:
time: 645 us; the launch traced here: 644 us
  waiting for transfers between devices  410 us (64%)
  blocking collectives  170 us (26%)
  matrix products  29 us (4%)
  between operations  14.6 us (2%)
  other arithmetic  11.7 us (2%)
  local copies, waits for them, and re-layouts  8.88 us (1%)
    reduce_scatter x1, waiting for transfers between devices, body(): lax.psum_scatter(jnp.einsum('slf,fd->lsd', score_gradient, upstream_signa...  209 us
    psum x1, waiting for transfers between devices, body(): context = lax.psum(value_partial, 'frame')  157 us
    pmax x1, blocking collectives, body(): row_max = lax.pmax(local_max, 'frame')  71.4 us
    all_gather x1, blocking collectives, body(): whole = lax.all_gather(texts, 'frame', axis=1, tiled=True)  49.8 us
    psum x1, blocking collectives, body(): loss = lax.psum(jnp.sum(loss_part), 'rec')  49.1 us
    all_gather x1, waiting for transfers between devices, body(): lax.all_gather(whole, 'rec', axis=0, tiled=True)  43.4 us
  transfers between devices with their start and end apart: 3, of which 3 were waited for; matrix products, arithmetic and copies ran while one was open for 2% of the time, Pallas kernels for 0%

commit v1 on v0

--- a/solution.py
+++ b/solution.py
@@ -69,7 +69,11 @@
     query_f = query_vectors.astype(jnp.float32)
     q_norm = lax.rsqrt(jnp.sum(query_f * query_f, axis=2) + EPS)
     q_unit = query_f * q_norm[..., None]
-    context = lax.psum(value_partial, "frame")
+    n_dev = lax.axis_size("frame")
+    context, reach = (value_partial, 1)
+    while reach < n_dev:
+        context = context + lax.ppermute(context, "frame", [(i, i ^ reach) for i in range(n_dev)])
+        reach = 2 * reach
     c_norm = lax.rsqrt(jnp.sum(context * context, axis=2) + EPS)
     c_unit = context * c_norm[..., None]
     cos = jnp.sum(q_unit * c_unit, axis=2)

time: 645 us -> 614 us (0.952)
  waiting for transfers between devices: 410 us -> 368 us
  starting transfers between devices: 0.3 us -> 18.4 us
    reduce_scatter x1 -> x0, waiting for transfers between devices: 209 us -> none  [body(): lax.psum_scatter(jnp.einsum('slf,fd->lsd', score_gradient, upstream_signa...]
    unnamed x3, waiting for transfers between devices: 0.05 us -> 166 us
    ppermute x0 -> x5, waiting for transfers between devices: none -> 158 us  [body(): lax.ppermute(context, 'frame', [(i, i ^ reach) for i in range(n_dev)])]
    psum x1 -> x0, waiting for transfers between devices: 157 us -> none  [body(): context = lax.psum(value_partial, 'frame')]
    ppermute x0 -> x5, starting transfers between devices: none -> 18.4 us  [body(): lax.ppermute(context, 'frame', [(i, i ^ reach) for i in range(n_dev)])]
  transfers between devices with their start and end apart: 3 -> 7, of which waited for: 3 -> 7; matrix products, arithmetic and copies ran while one was open for 2% -> 2% of each run, Pallas kernels for 0% -> 0%
where the time goes in v1:
time: 614 us
  waiting for transfers between devices  368 us (60%)
  blocking collectives  170 us (28%)
  matrix products  26.3 us (4%)
  starting transfers between devices  18.4 us (3%)
  between operations  15.5 us (3%)
  other arithmetic  8.49 us (1%)
  local copies, waits for them, and re-layouts  6.54 us (1%)
    unnamed x3, waiting for transfers between devices  166 us
    ppermute x5, waiting for transfers between devices, body(): lax.ppermute(context, 'frame', [(i, i ^ reach) for i in range(n_dev)])  158 us
    pmax x1, blocking collectives, body(): row_max = lax.pmax(local_max, 'frame')  71.3 us
    all_gather x1, blocking collectives, body(): whole = lax.all_gather(texts, 'frame', axis=1, tiled=True)  49.8 us
    psum x1, blocking collectives, body(): loss = lax.psum(jnp.sum(loss_part), 'rec')  49.1 us
    all_gather x1, waiting for transfers between devices, body(): lax.all_gather(whole, 'rec', axis=0, tiled=True)  43.8 us
    ppermute x5, starting transfers between devices, body(): lax.ppermute(context, 'frame', [(i, i ^ reach) for i in range(n_dev)])  18.4 us
  transfers between devices with their start and end apart: 7, of which 7 were waited for; matrix products, arithmetic and copies ran while one was open for 2% of the time, Pallas kernels for 0%

profile of v1, /device:TPU:16, one launch (start us, length us, event | category | flops | bytes accessed | tf_op | source)
XLA Modules:
  0.0 613.8 jit_solution(13758705461403345661)
XLA Ops:
  7.2 49.8 %all_gather.6 = bf16[2,224,256]{2,0,1:T(2,128)(2,1)S(1)} all-gather(bf16[2,7,256]{2,0,1:T(2,128)(2,1)} %param.6), channel_id=1, replica_groups=mesh['rec'=16,'frame'=32] {'frame'}, dimensions={1}, use_global_device_ids=true | all-gather | bytes 236544 | tf_op jit(solution)/shard_map/all_gather | solution.py:47
  57.0 0.7 copy.51
  57.8 0.9 select_reduce_fusion
  60.1 0.8 select_reduce_fusion.2
  60.9 43.8 %all-gather.2.cloned.1.call-done = bf16[32,224,256]{2,1,0:T(8,128)(2,1)} async-done(((bf16[2,224,256]{2,1,0:T(8,128)(2,1)}), bf16[32,224,256]{2,1,0:T(8,128)(2,1)}) %all-gather.2.cloned.1.call-update) | async-done | bytes 3670032 | tf_op jit(solution)/shard_map/all_gather | solution.py:51
  104.7 4.1 fusion.1
  109.2 4.4 multiply_reduce_fusion
  113.6 71.3 %pmax.7 = f32[6,224]{1,0:T(8,128)S(1)} all-reduce(f32[6,224]{1,0:T(8,128)S(1)} %get-tuple-element.19), channel_id=1, replica_groups=mesh['rec'=16,'frame'=32] {'frame'}, use_global_device_ids=true, to_apply=%region_6.0 | all-reduce | flops 1344 | bytes 10752 | tf_op jit(solution)/shard_map/pmax | solution.py:63
  185.0 4.8 fusion.9
  189.8 1.9 collective-permute-start
  191.8 24.7 %collective-permute-done = f32[6,224,256]{2,1,0:T(8,128)S(1)} collective-permute-done((f32[6,224,256]{2,1,0:T(8,128)S(1)}, f32[6,224,256]{2,1,0:T(8,128)S(1)}, u32[]{:S(2)}, u32[]{:S(2)}) %collective-permute-start) | collective-permute-done | bytes 1376288 | tf_op jit(solution)/shard_map/ppermute | solution.py:75
  216.7 8.2 %collective-permute-start.1 = (f32[6,224,256]{2,1,0:T(8,128)S(1)}, f32[6,224,256]{2,1,0:T(8,128)S(1)}, u32[]{:S(2)}, u32[]{:S(2)}) collective-permute-start(f32[6,224,256]{2,1,0:T(8,128)S(1)} %add.65), channel_id=1, source_target_pairs={{0,2},{1,3},{2,0},{3,1},{4,6},{5,7},{6,4},{7,5},{8,10},{9,11},{10,... | collective-permute-start | bytes 4128776 | tf_op jit(solution)/shard_map/ppermute | solution.py:75
  224.9 66.3 %collective-permute-done.1 = f32[6,224,256]{2,1,0:T(8,128)S(1)} collective-permute-done((f32[6,224,256]{2,1,0:T(8,128)S(1)}, f32[6,224,256]{2,1,0:T(8,128)S(1)}, u32[]{:S(2)}, u32[]{:S(2)}) %collective-permute-start.1) | collective-permute-done | bytes 1376288 | tf_op jit(solution)/shard_map/ppermute | solution.py:75
  291.4 1.9 collective-permute-start.2
  293.3 31.4 %collective-permute-done.2 = f32[6,224,256]{2,1,0:T(8,128)S(1)} collective-permute-done((f32[6,224,256]{2,1,0:T(8,128)S(1)}, f32[6,224,256]{2,1,0:T(8,128)S(1)}, u32[]{:S(2)}, u32[]{:S(2)}) %collective-permute-start.2) | collective-permute-done | bytes 1376288 | tf_op jit(solution)/shard_map/ppermute | solution.py:75
  324.9 1.9 collective-permute-start.3
  326.8 18.3 %collective-permute-done.3 = f32[6,224,256]{2,1,0:T(8,128)S(1)} collective-permute-done((f32[6,224,256]{2,1,0:T(8,128)S(1)}, f32[6,224,256]{2,1,0:T(8,128)S(1)}, u32[]{:S(2)}, u32[]{:S(2)}) %collective-permute-start.3) | collective-permute-done | bytes 1376288 | tf_op jit(solution)/shard_map/ppermute | solution.py:75
  345.3 4.4 collective-permute-start.4
  349.7 17.5 %collective-permute-done.4 = f32[6,224,256]{2,1,0:T(8,128)S(1)} collective-permute-done((f32[6,224,256]{2,1,0:T(8,128)S(1)}, f32[6,224,256]{2,1,0:T(8,128)S(1)}, u32[]{:S(2)}, u32[]{:S(2)}) %collective-permute-start.4) | collective-permute-done | bytes 1376288 | tf_op jit(solution)/shard_map/ppermute | solution.py:75
  367.6 0.8 multiply_reduce_fusion.2
  369.0 1.6 multiply_convert_fusion.1
  370.6 2.3 multiply_convert_fusion
  372.9 2.0 copy-done.1
  374.9 2.3 convolution_bitcast_fusion.2
  377.3 1.2 dynamic-slice.2
  378.5 1.3 dynamic-slice
  381.0 0.7 constant_dynamic-slice_fusion
  381.7 5.4 convolution_bitcast_fusion
  387.1 2.4 fusion.5
  389.5 166.2 %all-reduce.6.cloned.1.call-done = f32[224,6,256]{2,0,1:T(8,128)} async-done(((f32[224,6,256]{2,0,1:T(8,128)}), f32[224,6,256]{2,0,1:T(8,128)}) %all-reduce.6.cloned.1.call-update) | async-done | bytes 1376272
  555.7 1.0 fusion.20
  557.2 49.1 %all-reduce.7 = (f32[]{:T(128)}, bf16[32,7,256]{2,0,1:T(8,128)(2,1)S(1)}) all-reduce(f32[]{:T(128)} %get-tuple-element.18, f32[32,7,256]{2,0,1:T(8,128)S(1)} %fusion.15), channel_id=1, replica_groups=mesh['rec'=16,'frame'=32] {'rec'}, use_global_device_ids=true, to_apply=%region_10.11 | all-reduce | flops 57345 | bytes 344072 | tf_op jit(solution)/shard_map/psum | solution.py:113
  (48 shorter events, 4.6 us)
Async XLA Ops:
  7.2 102.0 %copy-start = (bf16[1,1536,256]{2,1,0:T(8,128)(2,1)S(1)}, bf16[1,1536,256]{2,1,0:T(8,128)(2,1)}, u32[]{:S(2)}) copy-start(bf16[1,1536,256]{2,1,0:T(8,128)(2,1)} %param.5) | copy-start | bytes 2359300
  7.2 97.5 %all-gather.2.cloned.1.call-start = ((), (), s32[]{:S(2)}) async-start(), calls=%async_computation | async-start | bytes 3899392 | tf_op jit(solution)/shard_map/all_gather | solution.py:51
  57.8 497.9 %all-reduce.6.cloned.1.call-start = ((), (), s32[]{:S(2)}) async-start(), calls=%async_computation.1 | async-start | bytes 2752512
  60.9 43.9 %copy-start.7 = (s32[6]{0:T(128)}, s32[6]{0:T(128)S(1)}, u32[]{:S(2)}) copy-start(s32[6]{0:T(128)S(1)} %get-tuple-element.6) | copy-start | bytes 76
  60.9 43.8 %copy-start.11 = (pred[6]{0:T(512)(128)(4,1)}, pred[6]{0:T(512)(128)(4,1)S(1)}, u32[]{:S(2)}) copy-start(pred[6]{0:T(512)(128)(4,1)S(1)} %broadcast_compare_fusion) | copy-start | bytes 22
  184.9 4.9 copy-start.3
  189.8 26.6 %collective-permute-start = (f32[6,224,256]{2,1,0:T(8,128)S(1)}, f32[6,224,256]{2,1,0:T(8,128)S(1)}, u32[]{:S(2)}, u32[]{:S(2)}) collective-permute-start(f32[6,224,256]{2,1,0:T(8,128)S(1)} %fusion.9), channel_id=1, source_target_pairs={{0,1},{1,0},{2,3},{3,2},{4,5},{5,4},{6,7},{7,6},{8,9},{9,8},{10,11... | collective-permute-start | bytes 4128776 | tf_op jit(solution)/shard_map/ppermute | solution.py:75
  216.7 74.5 %collective-permute-start.1 = (f32[6,224,256]{2,1,0:T(8,128)S(1)}, f32[6,224,256]{2,1,0:T(8,128)S(1)}, u32[]{:S(2)}, u32[]{:S(2)}) collective-permute-start(f32[6,224,256]{2,1,0:T(8,128)S(1)} %add.65), channel_id=1, source_target_pairs={{0,2},{1,3},{2,0},{3,1},{4,6},{5,7},{6,4},{7,5},{8,10},{9,11},{10,... | collective-permute-start | bytes 4128776 | tf_op jit(solution)/shard_map/ppermute | solution.py:75
  291.4 33.3 %collective-permute-start.2 = (f32[6,224,256]{2,1,0:T(8,128)S(1)}, f32[6,224,256]{2,1,0:T(8,128)S(1)}, u32[]{:S(2)}, u32[]{:S(2)}) collective-permute-start(f32[6,224,256]{2,1,0:T(8,128)S(1)} %add.66), channel_id=1, source_target_pairs={{0,4},{1,5},{2,6},{3,7},{4,0},{5,1},{6,2},{7,3},{8,12},{9,13},{10,... | collective-permute-start | bytes 4128776 | tf_op jit(solution)/shard_map/ppermute | solution.py:75
  324.9 20.2 %collective-permute-start.3 = (f32[6,224,256]{2,1,0:T(8,128)S(1)}, f32[6,224,256]{2,1,0:T(8,128)S(1)}, u32[]{:S(2)}, u32[]{:S(2)}) collective-permute-start(f32[6,224,256]{2,1,0:T(8,128)S(1)} %add.67), channel_id=1, source_target_pairs={{0,8},{1,9},{2,10},{3,11},{4,12},{5,13},{6,14},{7,15},{8,0},{9,1},... | collective-permute-start | bytes 4128776 | tf_op jit(solution)/shard_map/ppermute | solution.py:75
  345.1 25.5 %slice-start = ((s8[8257536]{0:T(1024)(128)(4,1)}), s8[4194304]{0:T(1024)(128)(4,1)S(1)}, s32[]{:S(2)}) async-start(s8[8257536]{0:T(1024)(128)(4,1)} %bitcast.46), calls=%async_computation.2 | async-start | bytes 8388608
  345.3 22.0 %collective-permute-start.4 = (f32[6,224,256]{2,1,0:T(8,128)S(1)}, f32[6,224,256]{2,1,0:T(8,128)S(1)}, u32[]{:S(2)}, u32[]{:S(2)}) collective-permute-start(f32[6,224,256]{2,1,0:T(8,128)S(1)} %add.68), channel_id=1, source_target_pairs={{0,16},{1,17},{2,18},{3,19},{4,20},{5,21},{6,22},{7,23},{8,24},{9,... | collective-permute-start | bytes 4128776 | tf_op jit(solution)/shard_map/ppermute | solution.py:75
  349.7 20.9 %slice-start.1 = ((s8[8257536]{0:T(1024)(128)(4,1)}), s8[4063232]{0:T(1024)(128)(4,1)S(1)}, s32[]{:S(2)}) async-start(s8[8257536]{0:T(1024)(128)(4,1)} %bitcast.46), calls=%async_computation.3 | async-start | bytes 8126464
  369.0 1.6 copy-start.9
  369.0 1.6 copy-start.4
  372.9 2.0 copy-start.1
  381.7 5.4 copy-start.2
  387.1 168.6 %copy-start.5 = (f32[6,7]{1,0:T(8,128)S(1)}, f32[6,7]{1,0:T(8,128)}, u32[]{:S(2)}) copy-start(f32[6,7]{1,0:T(8,128)} %get-tuple-element.21) | copy-start | bytes 508
  387.1 168.6 %copy-start.6 = (f32[6,7]{1,0:T(8,128)S(1)}, f32[6,7]{1,0:T(8,128)}, u32[]{:S(2)}) copy-start(f32[6,7]{1,0:T(8,128)} %get-tuple-element.22) | copy-start | bytes 508
  387.1 168.6 %copy-start.10 = (f32[6]{0:T(128)S(1)}, f32[6]{0:T(128)}, u32[]{:S(2)}) copy-start(f32[6]{0:T(128)} %copy-done.9) | copy-start | bytes 76
  387.1 169.6 %copy-start.8 = (s32[6]{0:T(128)S(1)}, s32[6]{0:T(128)}, u32[]{:S(2)}) copy-start(s32[6]{0:T(128)} %copy-done.7) | copy-start | bytes 76
  387.1 169.6 %copy-start.12 = (pred[6]{0:T(512)(128)(4,1)S(1)}, pred[6]{0:T(512)(128)(4,1)}, u32[]{:S(2)}) copy-start(pred[6]{0:T(512)(128)(4,1)} %copy-done.11) | copy-start | bytes 22
Sparse Core Ops, SparseCore 0:
  57.9 46.7 all-gather.1
  377.4 178.2 all-reduce.5
